TPU v7x, 32 devices: a whole 2x2x4 slice. The times are simulated.
32 devices in a mesh: gx: 8 (over y, x, core), gy: 4 (over z).
Axes of the slice: x: 2, y: 2, z: 4, core: 2. Of those that a mesh axis runs over, the one named last changes fastest.
Arguments:
- checkpoint: float32 [19, 64, 256, 128], P(None, 'gx', 'gy'), may hold values from 0 to 1, as said below
- fluid: int32 [64, 256, 128], P('gx', 'gy'), may hold values 0 or 1
- adjoint_in: float32 [19, 64, 256, 128], P(None, 'gx', 'gy'), may hold values from -6 to 6
Outputs:
- state: float32 [19, 64, 256, 128], P(None, 'gx', 'gy')
- adjoint: float32 [19, 64, 256, 128], P(None, 'gx', 'gy')
Inputs may be any that keep to these rules, and one draw needn't show every extreme that they name: `checkpoint`: positive populations near equilibrium. 1 marks a fluid cell, 0 a solid one.
All inputs are finite; a program needn't handle non-finite values. No bound on the sum of `fluid` on one device may be relied on, other than what follows from the above.
Results may differ from a plain program's by a relative error of at most 0.0003.
Values sent between devices are 32-bit elements; how exact they have to be, the bound alone decides.
A program may use at most 128 MiB of HBM per device.

v0:
```python
import jax
import jax.numpy as jnp
from jax import lax
from jax.experimental import pallas as pl
from jax.experimental.pallas import tpu as pltpu
from jax.sharding import PartitionSpec as P

VELOCITY = [
    (0, 0, 0),
    (1, 0, 0),
    (-1, 0, 0),
    (0, 1, 0),
    (0, -1, 0),
    (0, 0, 1),
    (0, 0, -1),
    (1, 1, 0),
    (-1, -1, 0),
    (1, -1, 0),
    (-1, 1, 0),
    (1, 0, 1),
    (-1, 0, -1),
    (1, 0, -1),
    (-1, 0, 1),
    (0, 1, 1),
    (0, -1, -1),
    (0, 1, -1),
    (0, -1, 1),
]
OPPOSITE = [0, 2, 1, 4, 3, 6, 5, 8, 7, 10, 9, 12, 11, 14, 13, 16, 15, 18, 17]
ORDER = [0, 1, 7, 9, 11, 13, 2, 8, 10, 12, 14, 3, 4, 5, 6, 15, 16, 17, 18]
SLOT = [ORDER.index(q) for q in range(19)]
UP = [3, 7, 10, 15, 17]
DOWN = [4, 8, 9, 16, 18]
CORNER = [7, 8, 9, 10]
PAD = 8
T = 8
MIB = 1 << 20


def shifted(ref, q, x, y, speed):
    row = PAD + T * y - speed[1]
    tile = ref[SLOT[q], x + 1 - speed[0], row : row + T, :]
    if speed[2]:
        tile = pltpu.roll(tile, speed[2] % tile.shape[1], 1)
    return tile


def own(ref, q, x, y):
    return ref[SLOT[q], x + 1, PAD + T * y : PAD + T * y + T, :]


def stream(ref, bits, x, y):
    result = [own(ref, 0, x, y)]
    for q in range(1, 19):
        is_open = (bits & (1 << q)) != 0
        result.append(
            jnp.where(is_open, shifted(ref, q, x, y, VELOCITY[q]), own(ref, OPPOSITE[q], x, y))
        )
    return result


def moments(v):
    s = {q: v[q] + v[q + 1] for q in range(1, 19, 2)}
    d = {q: v[q] - v[q + 1] for q in range(1, 19, 2)}
    rho = v[0] + ((s[1] + s[3]) + (s[5] + s[7])) + ((s[9] + s[11]) + (s[13] + (s[15] + s[17])))
    mx = d[1] + (d[7] + d[9]) + (d[11] + d[13])
    my = d[3] + (d[7] - d[9]) + (d[15] + d[17])
    mz = d[5] + (d[11] - d[13]) + (d[15] - d[17])
    return rho, mx, my, mz


def collide(v):
    rho, mx, my, mz = moments(v)
    inverse = 3.0 / rho
    ux, uy, uz = mx * inverse, my * inverse, mz * inverse
    base = 1.0 - (ux * ux + uy * uy + uz * uz) * (1.0 / 6.0)
    along = {
        1: ux,
        3: uy,
        5: uz,
        7: ux + uy,
        9: ux - uy,
        11: ux + uz,
        13: ux - uz,
        15: uy + uz,
        17: uy - uz,
    }
    axis, diagonal = rho * (1.6 / 18.0), rho * (1.6 / 36.0)
    result = [rho * (1.6 / 3.0) * base - 0.6 * v[0]]
    for q in range(1, 19, 2):
        a = along[q]
        even = base + 0.5 * (a * a)
        factor = axis if q < 7 else diagonal
        result.append(factor * (even + a) - 0.6 * v[q])
        result.append(factor * (even - a) - 0.6 * v[q + 1])
    return result


def pull_back(v, b):
    rho, mx, my, mz = moments(v)
    inverse = 1.0 / rho
    ux, uy, uz = mx * inverse, my * inverse, mz * inverse
    s = {q: b[q] + b[q + 1] for q in range(1, 19, 2)}
    d = {q: b[q] - b[q + 1] for q in range(1, 19, 2)}
    for q in (1, 3, 5):
        s[q] = s[q] + s[q]
        d[q] = d[q] + d[q]
    sxy_p, sxz_p, syz_p = s[7] + s[9], s[11] + s[13], s[15] + s[17]
    sxy, sxz, syz = s[7] - s[9], s[11] - s[13], s[15] - s[17]
    s0 = 12.0 * b[0] + (s[1] + s[3]) + (s[5] + sxy_p) + (sxz_p + syz_p)
    sxx, syy, szz = s[1] + sxy_p + sxz_p, s[3] + sxy_p + syz_p, s[5] + sxz_p + syz_p
    s1x = d[1] + (d[7] + d[9]) + (d[11] + d[13])
    s1y = d[3] + (d[7] - d[9]) + (d[15] + d[17])
    s1z = d[5] + (d[11] - d[13]) + (d[15] - d[17])
    tx = sxx * ux + sxy * uy + sxz * uz
    ty = sxy * ux + syy * uy + syz * uz
    tz = sxz * ux + syz * uy + szz * uz
    k = 1.6 / 36.0
    square = ux * ux + uy * uy + uz * uz
    level = k * (s0 * (1.0 + 1.5 * square) - 4.5 * (ux * tx + uy * ty + uz * tz))
    gx = (3.0 * k) * (s1x + 3.0 * tx - ux * s0)
    gy = (3.0 * k) * (s1y + 3.0 * ty - uy * s0)
    gz = (3.0 * k) * (s1z + 3.0 * tz - uz * s0)
    along = {
        1: gx,
        3: gy,
        5: gz,
        7: gx + gy,
        9: gx - gy,
        11: gx + gz,
        13: gx - gz,
        15: gy + gz,
        17: gy - gz,
    }
    result = [level - 0.6 * b[0]]
    for q in range(1, 19, 2):
        result.append((level + along[q]) - 0.6 * b[q])
        result.append((level - along[q]) - 0.6 * b[q + 1])
    return result


def forward_kernel(
    start_ref, fluid_ref, seed_ref,
    state_ref, adjoint_ref,
    post_a, held, bits_ref, post_b, start, cells, solid, y_send, y_recv, c_send, c_recv,
    load_sem, send_sem, recv_sem, seed_send, seed_recv,
):
    _, nx, ny, nz = start_ref.shape
    tiles = ny // T
    last = tiles - 1
    top = PAD + ny
    me = {"gx": lax.axis_index("gx"), "gy": lax.axis_index("gy")}
    count = {"gx": lax.axis_size("gx"), "gy": lax.axis_size("gy")}

    def device(dx, dy):
        to_x = lax.rem(me["gx"] + dx + count["gx"], count["gx"])
        to_y = lax.rem(me["gy"] + dy + count["gy"], count["gy"])
        return (to_x, to_y)

    around = [(i, j) for i in (-1, 0, 1) for j in (-1, 0, 1) if (i, j) != (0, 0)]
    barrier = pltpu.get_barrier_semaphore()
    for i, j in around:
        pl.semaphore_signal(barrier, inc=1, device_id=device(i, j), device_id_type=pl.DeviceIdType.MESH)

    fluid_load = pltpu.make_async_copy(fluid_ref, cells, load_sem.at[0])
    fluid_load.start()
    start_load = [
        pltpu.make_async_copy(start_ref.at[:, pl.ds(a, n)], start.at[:, pl.ds(a, n)], load_sem.at[1 + i])
        for i, (a, n) in enumerate(((0, 1), (nx - 1, 1), (1, nx - 2)))
    ]
    for load in start_load:
        load.start()
    seed_load = [
        pltpu.make_async_copy(
            seed_ref.at[q],
            held.at[SLOT[OPPOSITE[q]], pl.ds(1, nx), pl.ds(PAD, ny)],
            load_sem.at[4 + q],
        )
        for q in range(19)
    ]
    pl.semaphore_wait(barrier, len(around))
    seed_faces = []
    for i, (plane, halo, first_slot) in enumerate(((nx - 1, 0, 1), (0, nx + 1, 6))):
        for k in range(5):
            slot = first_slot + k
            seed_faces.append(
                pltpu.make_async_remote_copy(
                    src_ref=seed_ref.at[OPPOSITE[ORDER[slot]], plane],
                    dst_ref=held.at[slot, halo, pl.ds(PAD, ny)],
                    send_sem=seed_send.at[i, k],
                    recv_sem=seed_recv.at[i, k],
                    device_id=device(1 - 2 * i, 0),
                    device_id_type=pl.DeviceIdType.MESH,
                )
            )

    def copies(e, ref, is_cells, first_of=0):
        made = []
        for i, (plane, halo, first) in enumerate(((nx, 0, 1), (1, nx + 1, 6))):
            rows = pl.ds(PAD, ny)
            if is_cells:
                source, target = ref.at[plane, rows], ref.at[halo, rows]
            else:
                five = pl.ds(first, 5)
                source, target = ref.at[five, plane, rows], ref.at[five, halo, rows]
            made.append((source, target, device(1 - 2 * i, 0)))
        for i in range(2):
            made.append((y_send.at[e, i], y_recv.at[e, i], device(0, 1 - 2 * i)))
        for i, q in enumerate(CORNER):
            made.append((c_send.at[e, i], c_recv.at[e, i], device(VELOCITY[q][0], VELOCITY[q][1])))
        return [
            pltpu.make_async_remote_copy(
                src_ref=source, dst_ref=target, send_sem=send_sem.at[e, i], recv_sem=recv_sem.at[e, i],
                device_id=to, device_id_type=pl.DeviceIdType.MESH,
            )
            for i, (source, target, to) in enumerate(made)
            if i >= first_of
        ]

    def pack(e, ref):
        def one(x, _):
            for k in range(5):
                y_send[e, 0, k, x] = ref[SLOT[UP[k]], x + 1, top - 1 : top, :]
                y_send[e, 1, k, x] = ref[SLOT[DOWN[k]], x + 1, PAD : PAD + 1, :]
            return 0

        lax.fori_loop(0, nx, one, 0)
        for i, q in enumerate(CORNER):
            plane = nx if VELOCITY[q][0] == 1 else 1
            row = top - 1 if VELOCITY[q][1] == 1 else PAD
            c_send[e, i] = ref[SLOT[q], plane, row : row + 1, :]

    def unpack(e, ref):
        def one(x, _):
            for k in range(5):
                ref[SLOT[UP[k]], x + 1, PAD - 1 : PAD, :] = y_recv[e, 0, k, x]
                ref[SLOT[DOWN[k]], x + 1, top : top + 1, :] = y_recv[e, 1, k, x]
            return 0

        lax.fori_loop(0, nx, one, 0)
        for i, q in enumerate(CORNER):
            plane = 0 if VELOCITY[q][0] == 1 else nx + 1
            row = PAD - 1 if VELOCITY[q][1] == 1 else top
            ref[SLOT[q], plane, row : row + 1, :] = c_recv[e, i]

    def sweep_faces(body):
        def face(i, _):
            for y in range(tiles):
                body(i * (nx - 1), y)
            return 0

        lax.fori_loop(0, 2, face, 0)

    def sweep_edges(body):
        def edge(x, _):
            body(x, 0)
            body(x, last)
            return 0

        lax.fori_loop(1, nx - 1, edge, 0)

    def sweep_interior(body):
        def line(x, _):
            for y in range(1, last):
                body(x, y)
            return 0

        lax.fori_loop(1, nx - 1, line, 0)

    def begin(made):
        for copy in made:
            copy.start()

    def finish(made):
        for copy in made:
            copy.wait()

    fluid_load.wait()

    def to_float(x, _):
        solid[x + 1, PAD:top, :] = cells[x].astype(jnp.float32)
        y_send[0, 0, 0, x] = solid[x + 1, top - 1 : top, :]
        y_send[0, 1, 0, x] = solid[x + 1, PAD : PAD + 1, :]
        for k in range(1, 5):
            y_send[0, 0, k, x] = jnp.zeros((1, nz), jnp.float32)
            y_send[0, 1, k, x] = jnp.zeros((1, nz), jnp.float32)
        return 0

    lax.fori_loop(0, nx, to_float, 0)
    for i, q in enumerate(CORNER):
        plane = nx if VELOCITY[q][0] == 1 else 1
        row = top - 1 if VELOCITY[q][1] == 1 else PAD
        c_send[0, i] = solid[plane, row : row + 1, :]
    cell_copies = copies(0, solid, True)
    begin(cell_copies)

    def store(to, x, y, v, is_fluid):
        for q, value in enumerate(collide(v)):
            to[SLOT[q], x + 1, PAD + T * y : PAD + T * y + T, :] = jnp.where(
                is_fluid, value, v[OPPOSITE[q]]
            )

    def first(x, y):
        v = [start[q, x, T * y : T * y + T, :] for q in range(19)]
        store(post_a, x, y, v, solid[x + 1, PAD + T * y : PAD + T * y + T, :] > 0.5)

    for load in start_load[:2]:
        load.wait()
    first_copies = copies(1, post_a, False)
    sweep_faces(first)
    begin(first_copies[:2])
    start_load[2].wait()
    for load in seed_load:
        load.start()
    sweep_edges(first)
    pack(1, post_a)
    begin(first_copies[2:])
    sweep_interior(first)

    for load in seed_load:
        load.wait()
    pack(4, held)
    seed_copies = copies(4, held, False, 2)
    begin(seed_copies)
    for copy in seed_faces:
        copy.start()

    finish(cell_copies)

    def place_cells(x, _):
        solid[x + 1, PAD - 1 : PAD, :] = y_recv[0, 0, 0, x]
        solid[x + 1, top : top + 1, :] = y_recv[0, 1, 0, x]
        return 0

    lax.fori_loop(0, nx, place_cells, 0)
    for i, q in enumerate(CORNER):
        plane = 0 if VELOCITY[q][0] == 1 else nx + 1
        row = PAD - 1 if VELOCITY[q][1] == 1 else top
        solid[plane, row : row + 1, :] = c_recv[0, i]

    layer = lax.broadcasted_iota(jnp.int32, (T, nz), 1)
    inside = {1: (layer > 0).astype(jnp.float32), -1: (layer < nz - 1).astype(jnp.float32)}

    def mark(x, _):
        for y in range(tiles):
            flat, up, down = 1.0, 0.0, 0.0
            for q in range(1, 19):
                c = VELOCITY[q]
                row = PAD + T * y - c[1]
                tile = solid[x + 1 - c[0], row : row + T, :] * float(1 << q)
                if c[2] == 0:
                    flat = flat + tile
                elif c[2] == 1:
                    up = up + tile
                else:
                    down = down + tile
            total = flat + pltpu.roll(up, 1, 1) * inside[1] + pltpu.roll(down, nz - 1, 1) * inside[-1]
            here = solid[x + 1, PAD + T * y : PAD + T * y + T, :]
            bits_ref[x, T * y : T * y + T, :] = (total * here).astype(jnp.int32)
        return 0

    lax.fori_loop(0, nx, mark, 0)

    def middle(source, to):
        def body(x, y):
            bits = bits_ref[x, T * y : T * y + T, :]
            v = stream(source, bits, x, y)
            store(to, x, y, v, (bits & 1) != 0)

        return body

    def step(e, made, source, to):
        body = middle(source, to)
        sweep_interior(body)
        finish(made[2:])
        unpack(e, source)
        sweep_edges(body)
        finish(made[:2])
        sweep_faces(body)
        later = copies(e + 1, to, False)
        begin(later[:2])
        pack(e + 1, to)
        begin(later[2:])
        return later

    second_copies = step(1, first_copies, post_a, post_b)
    third_copies = step(2, second_copies, post_b, post_a)
    finish(seed_copies)
    unpack(4, held)

    def final(x, y):
        rows = slice(T * y, T * y + T)
        bits = bits_ref[x, rows, :]
        v = stream(post_a, bits, x, y)
        for q in range(19):
            state_ref[q, x, rows, :] = v[q]
        turned = stream(held, bits, x, y)
        through = pull_back(v, [turned[OPPOSITE[q]] for q in range(19)])
        is_fluid = (bits & 1) != 0
        for q in range(19):
            adjoint_ref[q, x, rows, :] = jnp.where(is_fluid, through[q], turned[q])

    sweep_interior(final)
    finish(third_copies[2:])
    unpack(3, post_a)
    sweep_edges(final)
    finish(third_copies[:2])
    finish(seed_faces)
    sweep_faces(final)


def write_kernel(state_in, adjoint_in, state_ref, adjoint_ref, sem):
    made = []
    for i, (source, target) in enumerate(((state_in, state_ref), (adjoint_in, adjoint_ref))):
        for q in range(source.shape[0]):
            made.append(pltpu.make_async_copy(source.at[q], target.at[q], sem.at[i, q]))
    for copy in made:
        copy.start()
    for copy in made:
        copy.wait()


def per_device(checkpoint, fluid, adjoint_in):
    n, nx, ny, nz = checkpoint.shape
    padded = (n, nx + 2, ny + 2 * PAD, nz)
    f32 = jnp.float32
    state, adjoint = pl.pallas_call(
        forward_kernel,
        out_shape=(
            pltpu.VMEM((n, nx, ny, nz), f32),
            pltpu.VMEM((n, nx, ny, nz), f32),
        ),
        in_specs=[pl.BlockSpec(memory_space=pltpu.HBM)] * 3,
        out_specs=[pl.BlockSpec(memory_space=pltpu.VMEM)] * 2,
        scratch_shapes=[
            pltpu.VMEM(padded, f32),
            pltpu.VMEM(padded, f32),
            pltpu.VMEM((nx, ny, nz), jnp.int32),
            pltpu.VMEM(padded, f32),
            pltpu.VMEM((n, nx, ny, nz), f32),
            pltpu.VMEM((nx, ny, nz), jnp.int32),
            pltpu.VMEM(padded[1:], f32),
            pltpu.VMEM((5, 2, 5, nx, 1, nz), f32),
            pltpu.VMEM((5, 2, 5, nx, 1, nz), f32),
            pltpu.VMEM((5, 4, 1, nz), f32),
            pltpu.VMEM((5, 4, 1, nz), f32),
            pltpu.SemaphoreType.DMA((23,)),
            pltpu.SemaphoreType.DMA((5, 8)),
            pltpu.SemaphoreType.DMA((5, 8)),
            pltpu.SemaphoreType.DMA((2, 5)),
            pltpu.SemaphoreType.DMA((2, 5)),
        ],
        compiler_params=pltpu.CompilerParams(
            collective_id=0, has_side_effects=True, vmem_limit_bytes=50 * MIB
        ),
        name="forward",
    )(checkpoint, fluid, adjoint_in)
    return pl.pallas_call(
        write_kernel,
        out_shape=(jax.ShapeDtypeStruct((n, nx, ny, nz), f32),) * 2,
        in_specs=[pl.BlockSpec(memory_space=pltpu.VMEM)] * 2,
        out_specs=[pl.BlockSpec(memory_space=pl.ANY)] * 2,
        scratch_shapes=[pltpu.SemaphoreType.DMA((2, n))],
        compiler_params=pltpu.CompilerParams(vmem_limit_bytes=4 * MIB),
        name="write",
    )(state, adjoint)


def solution(mesh):
    return jax.shard_map(
        per_device,
        mesh=mesh,
        in_specs=(P(None, "gx", "gy", None), P("gx", "gy", None), P(None, "gx", "gy", None)),
        out_specs=(P(None, "gx", "gy", None), P(None, "gx", "gy", None)),
        check_vma=False,
    )
```

profile of v0, /device:TPU:0, one launch (start us, length us, event | category | flops | bytes accessed | tf_op | source)
XLA Modules:
  0.0 33.7 jit_solution(12304948727227154671)
XLA Ops:
  0.6 29.0 %forward.1 = (f32[19,8,64,128]{3,2,1,0:T(8,128)S(1)}, f32[19,8,64,128]{3,2,1,0:T(8,128)S(1)}) custom-call(f32[19,8,64,128]{3,2,1,0:T(8,128)} %start_ref.1, s32[8,64,128]{2,1,0:T(8,128)} %fluid_ref.1, f32[19,8,64,128]{3,2,1,0:T(8,128)} %seed_ref.1), custom_call_target="tpu_custom_call" | custom-call | tf_op jit(solution)/shard_map/forward/pallas_call | solution.py:427
  29.6 4.1 %write.1 = (f32[19,8,64,128]{3,2,1,0:T(8,128)}, f32[19,8,64,128]{3,2,1,0:T(8,128)}) custom-call(f32[19,8,64,128]{3,2,1,0:T(8,128)S(1)} %get-tuple-element.4.state_in, f32[19,8,64,128]{3,2,1,0:T(8,128)S(1)} %get-tuple-element.5.adjoint_in), custom_call_target="tpu_custom_call" | custom-call | tf_op jit(solution)/shard_map/write/pallas_call | solution.py:458
where the time goes:
time: 33.8 us; the launch traced here: 33.7 us
  Pallas kernels  33 us (98%)
  between operations  0.64 us (2%)
    pallas_call x1, Pallas kernels, per_device(): pl.pallas_call(forward_kernel, out_shape=(pltpu.VMEM((n, nx, ny, nz), f32...  29 us
    pallas_call x1, Pallas kernels, per_device(): pl.pallas_call(write_kernel, out_shape=(jax.ShapeDtypeStruct((n, nx, ny,...  4.07 us

commit v1 on v0

v1 whole, which is shorter than its diff:
```python
import jax
import jax.numpy as jnp
from jax import lax
from jax.experimental import pallas as pl
from jax.experimental.pallas import tpu as pltpu
from jax.sharding import PartitionSpec as P

VELOCITY = [
    (0, 0, 0),
    (1, 0, 0),
    (-1, 0, 0),
    (0, 1, 0),
    (0, -1, 0),
    (0, 0, 1),
    (0, 0, -1),
    (1, 1, 0),
    (-1, -1, 0),
    (1, -1, 0),
    (-1, 1, 0),
    (1, 0, 1),
    (-1, 0, -1),
    (1, 0, -1),
    (-1, 0, 1),
    (0, 1, 1),
    (0, -1, -1),
    (0, 1, -1),
    (0, -1, 1),
]
OPPOSITE = [0, 2, 1, 4, 3, 6, 5, 8, 7, 10, 9, 12, 11, 14, 13, 16, 15, 18, 17]
ORDER = [0, 1, 7, 9, 11, 13, 2, 8, 10, 12, 14, 3, 4, 5, 6, 15, 16, 17, 18]
SLOT = [ORDER.index(q) for q in range(19)]
UP = [3, 7, 10, 15, 17]
DOWN = [4, 8, 9, 16, 18]
CORNER = [7, 8, 9, 10]
PAD = 8
T = 8
MIB = 1 << 20


def shifted(ref, q, x, y, speed):
    row = PAD + T * y - speed[1]
    tile = ref[SLOT[q], x + 1 - speed[0], row : row + T, :]
    if speed[2]:
        tile = pltpu.roll(tile, speed[2] % tile.shape[1], 1)
    return tile


def own(ref, q, x, y):
    return ref[SLOT[q], x + 1, PAD + T * y : PAD + T * y + T, :]


def stream(ref, bits, x, y):
    result = [own(ref, 0, x, y)]
    for q in range(1, 19):
        is_open = (bits & (1 << q)) != 0
        result.append(
            jnp.where(is_open, shifted(ref, q, x, y, VELOCITY[q]), own(ref, OPPOSITE[q], x, y))
        )
    return result


def moments(v):
    s = {q: v[q] + v[q + 1] for q in range(1, 19, 2)}
    d = {q: v[q] - v[q + 1] for q in range(1, 19, 2)}
    rho = v[0] + ((s[1] + s[3]) + (s[5] + s[7])) + ((s[9] + s[11]) + (s[13] + (s[15] + s[17])))
    mx = d[1] + (d[7] + d[9]) + (d[11] + d[13])
    my = d[3] + (d[7] - d[9]) + (d[15] + d[17])
    mz = d[5] + (d[11] - d[13]) + (d[15] - d[17])
    return rho, mx, my, mz


def collide(v):
    rho, mx, my, mz = moments(v)
    inverse = 3.0 / rho
    ux, uy, uz = mx * inverse, my * inverse, mz * inverse
    base = 1.0 - (ux * ux + uy * uy + uz * uz) * (1.0 / 6.0)
    along = {
        1: ux,
        3: uy,
        5: uz,
        7: ux + uy,
        9: ux - uy,
        11: ux + uz,
        13: ux - uz,
        15: uy + uz,
        17: uy - uz,
    }
    axis, diagonal = rho * (1.6 / 18.0), rho * (1.6 / 36.0)
    result = [rho * (1.6 / 3.0) * base - 0.6 * v[0]]
    for q in range(1, 19, 2):
        a = along[q]
        even = base + 0.5 * (a * a)
        factor = axis if q < 7 else diagonal
        result.append(factor * (even + a) - 0.6 * v[q])
        result.append(factor * (even - a) - 0.6 * v[q + 1])
    return result


def pull_back(v, b):
    rho, mx, my, mz = moments(v)
    inverse = 1.0 / rho
    ux, uy, uz = mx * inverse, my * inverse, mz * inverse
    s = {q: b[q] + b[q + 1] for q in range(1, 19, 2)}
    d = {q: b[q] - b[q + 1] for q in range(1, 19, 2)}
    for q in (1, 3, 5):
        s[q] = s[q] + s[q]
        d[q] = d[q] + d[q]
    sxy_p, sxz_p, syz_p = s[7] + s[9], s[11] + s[13], s[15] + s[17]
    sxy, sxz, syz = s[7] - s[9], s[11] - s[13], s[15] - s[17]
    s0 = 12.0 * b[0] + (s[1] + s[3]) + (s[5] + sxy_p) + (sxz_p + syz_p)
    sxx, syy, szz = s[1] + sxy_p + sxz_p, s[3] + sxy_p + syz_p, s[5] + sxz_p + syz_p
    s1x = d[1] + (d[7] + d[9]) + (d[11] + d[13])
    s1y = d[3] + (d[7] - d[9]) + (d[15] + d[17])
    s1z = d[5] + (d[11] - d[13]) + (d[15] - d[17])
    tx = sxx * ux + sxy * uy + sxz * uz
    ty = sxy * ux + syy * uy + syz * uz
    tz = sxz * ux + syz * uy + szz * uz
    k = 1.6 / 36.0
    square = ux * ux + uy * uy + uz * uz
    level = k * (s0 * (1.0 + 1.5 * square) - 4.5 * (ux * tx + uy * ty + uz * tz))
    gx = (3.0 * k) * (s1x + 3.0 * tx - ux * s0)
    gy = (3.0 * k) * (s1y + 3.0 * ty - uy * s0)
    gz = (3.0 * k) * (s1z + 3.0 * tz - uz * s0)
    along = {
        1: gx,
        3: gy,
        5: gz,
        7: gx + gy,
        9: gx - gy,
        11: gx + gz,
        13: gx - gz,
        15: gy + gz,
        17: gy - gz,
    }
    result = [level - 0.6 * b[0]]
    for q in range(1, 19, 2):
        result.append((level + along[q]) - 0.6 * b[q])
        result.append((level - along[q]) - 0.6 * b[q + 1])
    return result


SLOW, FAST = 0, 1
LOW, HIGH, MIDDLE, OTHER, Y_SLOW, Y_REST, DIAGONAL = 0, 1, 2, 3, 4, 6, 8
LANES = 12


def forward_kernel(
    start_ref, fluid_ref, seed_ref,
    state_ref, adjoint_ref,
    post_1, post_2, post_3, held, bits_ref, start, cells, solid,
    y_send, y_recv, c_send, c_recv,
    load_sem, send_sem, recv_sem, seed_send, seed_recv,
):
    _, nx, ny, nz = start_ref.shape
    tiles = ny // T
    last = tiles - 1
    top = PAD + ny
    me = {"gx": lax.axis_index("gx"), "gy": lax.axis_index("gy")}
    count = {"gx": lax.axis_size("gx"), "gy": lax.axis_size("gy")}
    odd = lax.rem(me["gx"], 2)
    sign = {SLOW: odd, FAST: 1 - odd}
    face = {side: (nx - 1) * p for side, p in sign.items()}
    rest = pl.ds(1 - odd, nx - 1)

    def first_of(p):
        return 6 - 5 * p

    def corner_of(p, up):
        return 8 - 6 * p if up else 7 - 4 * p

    def halo_of(p):
        return (nx + 1) * (1 - p)

    def device(dx, dy):
        to_x = lax.rem(me["gx"] + dx + count["gx"], count["gx"])
        to_y = lax.rem(me["gy"] + dy + count["gy"], count["gy"])
        return (to_x, to_y)

    def toward(side, dy):
        return device(2 * sign[side] - 1, dy)

    around = [(i, j) for i in (-1, 0, 1) for j in (-1, 0, 1) if (i, j) != (0, 0)]
    barrier = pltpu.get_barrier_semaphore()
    for i, j in around:
        pl.semaphore_signal(barrier, inc=1, device_id=device(i, j), device_id_type=pl.DeviceIdType.MESH)

    fluid_load = pltpu.make_async_copy(fluid_ref, cells, load_sem.at[0])
    fluid_load.start()
    start_load = [
        pltpu.make_async_copy(start_ref.at[:, planes], start.at[:, planes], load_sem.at[1 + i])
        for i, planes in enumerate((pl.ds(face[SLOW], 1), pl.ds(face[FAST], 1), pl.ds(1, nx - 2)))
    ]
    for load in start_load:
        load.start()
    seed_load = [
        pltpu.make_async_copy(
            seed_ref.at[q],
            held.at[SLOT[OPPOSITE[q]], pl.ds(1, nx), pl.ds(PAD, ny)],
            load_sem.at[4 + q],
        )
        for q in range(19)
    ]

    def remote(source, target, send, receive, to):
        return pltpu.make_async_remote_copy(
            src_ref=source, dst_ref=target, send_sem=send, recv_sem=receive,
            device_id=to, device_id_type=pl.DeviceIdType.MESH,
        )

    seed_faces = {
        side: [
            remote(
                seed_ref.at[2 * k + 5 + p if k else 1 + p, face[side]],
                held.at[first_of(p) + k, halo_of(p), pl.ds(PAD, ny)],
                seed_send.at[side, k], seed_recv.at[side, k], toward(side, 0),
            )
            for k in range(5)
        ]
        for side, p in sign.items()
    }

    def face_copy(e, lane, ref, side, first_tile, end_tile):
        p = sign[side]
        five, rows = pl.ds(first_of(p), 5), pl.ds(PAD + T * first_tile, T * (end_tile - first_tile))
        return remote(
            ref.at[five, face[side] + 1, rows], ref.at[five, halo_of(p), rows],
            send_sem.at[e, lane], recv_sem.at[e, lane], toward(side, 0),
        )

    def row_copies(e, lane, planes):
        return [
            remote(
                y_send.at[e, i, planes], y_recv.at[e, i, planes],
                send_sem.at[e, lane + i], recv_sem.at[e, lane + i], device(0, 1 - 2 * i),
            )
            for i in range(2)
        ]

    def corner_copies(e, side):
        return [
            remote(
                c_send.at[e, 2 * side + i], c_recv.at[e, 2 * side + i],
                send_sem.at[e, DIAGONAL + 2 * side + i], recv_sem.at[e, DIAGONAL + 2 * side + i],
                toward(side, 1 - 2 * i),
            )
            for i in range(2)
        ]

    def pack_plane(e, ref, x):
        for k in range(5):
            y_send[e, 0, x, k] = ref[SLOT[UP[k]], x + 1, top - 1 : top, :]
            y_send[e, 1, x, k] = ref[SLOT[DOWN[k]], x + 1, PAD : PAD + 1, :]

    def unpack_plane(e, ref, x):
        for k in range(5):
            ref[SLOT[UP[k]], x + 1, PAD - 1 : PAD, :] = y_recv[e, 0, x, k]
            ref[SLOT[DOWN[k]], x + 1, top : top + 1, :] = y_recv[e, 1, x, k]

    def sweep(begin_at, length, body):
        def one(i, _):
            body(begin_at + i)
            return 0

        lax.fori_loop(0, length, one, 0)

    def pack_corners(e, ref, side):
        p = sign[side]
        c_send[e, 2 * side] = ref[corner_of(p, True), face[side] + 1, top - 1 : top, :]
        c_send[e, 2 * side + 1] = ref[corner_of(p, False), face[side] + 1, PAD : PAD + 1, :]

    def unpack_corners(e, ref, side):
        p = 1 - sign[side]
        ref[corner_of(p, True), halo_of(p), PAD - 1 : PAD, :] = c_recv[e, 2 * side]
        ref[corner_of(p, False), halo_of(p), top : top + 1, :] = c_recv[e, 2 * side + 1]

    sent = []

    def begin(made):
        for copy in made:
            copy.start()
        sent.extend(made)

    def arrive(made):
        for copy in made:
            copy.wait_recv()

    fluid_load.wait()

    def to_float(x):
        solid[x + 1, PAD:top, :] = cells[x].astype(jnp.float32)
        y_send[0, 0, x, 0] = solid[x + 1, top - 1 : top, :]
        y_send[0, 1, x, 0] = solid[x + 1, PAD : PAD + 1, :]

    sweep(0, nx, to_float)
    for side in (SLOW, FAST):
        c_send[0, 2 * side] = solid[face[side] + 1, top - 1 : top, :]
        c_send[0, 2 * side + 1] = solid[face[side] + 1, PAD : PAD + 1, :]
    pl.semaphore_wait(barrier, len(around))
    cell_copies = [
        remote(
            solid.at[face[side] + 1, pl.ds(PAD, ny)], solid.at[halo_of(sign[side]), pl.ds(PAD, ny)],
            send_sem.at[0, side], recv_sem.at[0, side], toward(side, 0),
        )
        for side in (SLOW, FAST)
    ]
    for i in range(2):
        cell_copies.append(
            remote(
                y_send.at[0, i, :, 0], y_recv.at[0, i, :, 0],
                send_sem.at[0, Y_SLOW + i], recv_sem.at[0, Y_SLOW + i], device(0, 1 - 2 * i),
            )
        )
    cell_copies += corner_copies(0, SLOW) + corner_copies(0, FAST)
    begin(cell_copies)

    def store(to, x, y, v, is_fluid):
        for q, value in enumerate(collide(v)):
            to[SLOT[q], x + 1, PAD + T * y : PAD + T * y + T, :] = jnp.where(
                is_fluid, value, v[OPPOSITE[q]]
            )

    def first(x, y):
        v = [start[q, x, T * y : T * y + T, :] for q in range(19)]
        store(post_1, x, y, v, solid[x + 1, PAD + T * y : PAD + T * y + T, :] > 0.5)

    def middle(source, to):
        def body(x, y):
            bits = bits_ref[x, T * y : T * y + T, :]
            v = stream(source, bits, x, y)
            store(to, x, y, v, (bits & 1) != 0)

        return body

    def edge_line(body):
        def line(x):
            body(x, 0)
            body(x, last)

        return line

    def inner_line(body):
        def line(x):
            for y in range(1, last):
                body(x, y)

        return line

    def sweep_edges(body):
        sweep(1, nx - 2, edge_line(body))

    def sweep_interior(body):
        sweep(1, nx - 2, inner_line(body))

    def slow_copies(e, ref):
        outer = 4 - e
        return {
            "outer": [
                face_copy(e, LOW, ref, SLOW, 0, outer),
                face_copy(e, HIGH, ref, SLOW, tiles - outer, tiles),
            ],
            "middle": [face_copy(e, MIDDLE, ref, SLOW, outer, tiles - outer)],
            "corners": corner_copies(e, SLOW),
            "rows": row_copies(e, Y_SLOW, pl.ds(face[SLOW], 1)),
        }

    def send_outer(e, to, body):
        made = slow_copies(e, to)
        outer = 4 - e
        for i in range(outer):
            body(face[SLOW], i)
            body(face[SLOW], last - i)
            if i == 0:
                pack_corners(e, to, SLOW)
                pack_plane(e, to, face[SLOW])
                begin(made["corners"] + made["rows"])
        begin(made["outer"])
        return made

    def send_middle(e, made, body):
        outer = 4 - e
        for y in range(outer, tiles - outer):
            body(face[SLOW], y)
        begin(made["middle"])

    def other_copies(e, ref):
        return {
            "face": [face_copy(e, OTHER, ref, FAST, 0, tiles)] + corner_copies(e, FAST),
            "rows": row_copies(e, Y_REST, rest),
        }

    def send_fast(e, to, body):
        made = other_copies(e, to)
        for y in range(tiles):
            body(face[FAST], y)
        pack_corners(e, to, FAST)
        begin(made["face"])
        return made

    def send_rows(e, to, made):
        sweep(1 - odd, nx - 1, lambda x: pack_plane(e, to, x))
        begin(made["rows"])

    def take_rows(e, ref, slow, other):
        arrive(slow["rows"] + other["rows"])
        sweep(0, nx, lambda x: unpack_plane(e, ref, x))

    def take_fast(e, ref, made):
        arrive(made["face"])
        unpack_corners(e, ref, FAST)

    def take_outer(e, ref, made):
        arrive(made["corners"])
        unpack_corners(e, ref, SLOW)
        arrive(made["outer"])

    start_load[0].wait()
    slow_1 = send_outer(1, post_1, first)
    send_middle(1, slow_1, first)
    begin(seed_faces[SLOW][:2])
    start_load[1].wait()
    fast_1 = send_fast(1, post_1, first)
    start_load[2].wait()
    for load in seed_load:
        load.start()
    sweep_edges(first)
    send_rows(1, post_1, fast_1)
    sweep_interior(first)

    layer = lax.broadcasted_iota(jnp.int32, (T, nz), 1)
    inside = {1: (layer > 0).astype(jnp.float32), -1: (layer < nz - 1).astype(jnp.float32)}

    def mark(x, y):
        flat, up, down = 1.0, 0.0, 0.0
        for q in range(1, 19):
            c = VELOCITY[q]
            row = PAD + T * y - c[1]
            tile = solid[x + 1 - c[0], row : row + T, :] * float(1 << q)
            if c[2] == 0:
                flat = flat + tile
            elif c[2] == 1:
                up = up + tile
            else:
                down = down + tile
        total = flat + pltpu.roll(up, 1, 1) * inside[1] + pltpu.roll(down, nz - 1, 1) * inside[-1]
        here = solid[x + 1, PAD + T * y : PAD + T * y + T, :]
        bits_ref[x, T * y : T * y + T, :] = (total * here).astype(jnp.int32)

    sweep_interior(mark)
    second = middle(post_1, post_2)
    sweep_interior(second)

    for load in seed_load:
        load.wait()
    sweep(0, nx, lambda x: pack_plane(4, held, x))
    pack_corners(4, held, SLOW)
    pack_corners(4, held, FAST)
    seed_rims = row_copies(4, Y_SLOW, pl.ds(0, nx)) + corner_copies(4, SLOW) + corner_copies(4, FAST)
    begin(seed_rims)
    begin(seed_faces[FAST])

    arrive(cell_copies)

    def place_cells(x):
        solid[x + 1, PAD - 1 : PAD, :] = y_recv[0, 0, x, 0]
        solid[x + 1, top : top + 1, :] = y_recv[0, 1, x, 0]

    sweep(0, nx, place_cells)
    for side in (SLOW, FAST):
        halo = halo_of(1 - sign[side])
        solid[halo, PAD - 1 : PAD, :] = c_recv[0, 2 * side]
        solid[halo, top : top + 1, :] = c_recv[0, 2 * side + 1]
    sweep_edges(mark)

    def mark_face(i):
        for y in range(tiles):
            mark(i * (nx - 1), y)

    sweep(0, 2, mark_face)

    take_rows(1, post_1, slow_1, fast_1)
    sweep_edges(second)
    take_fast(1, post_1, fast_1)
    fast_2 = send_fast(2, post_2, second)
    send_rows(2, post_2, fast_2)
    take_outer(1, post_1, slow_1)
    slow_2 = send_outer(2, post_2, second)
    arrive(slow_1["middle"])
    send_middle(2, slow_2, second)
    begin(seed_faces[SLOW][2:4])

    third = middle(post_2, post_3)
    sweep_interior(third)
    take_rows(2, post_2, slow_2, fast_2)
    sweep_edges(third)
    take_fast(2, post_2, fast_2)
    fast_3 = send_fast(3, post_3, third)
    send_rows(3, post_3, fast_3)
    take_outer(2, post_2, slow_2)
    slow_3 = send_outer(3, post_3, third)
    begin(seed_faces[SLOW][4:])

    def final(x, y):
        rows = slice(T * y, T * y + T)
        bits = bits_ref[x, rows, :]
        v = stream(post_3, bits, x, y)
        for q in range(19):
            state_ref[q, x, rows, :] = v[q]
        turned = stream(held, bits, x, y)
        through = pull_back(v, [turned[OPPOSITE[q]] for q in range(19)])
        is_fluid = (bits & 1) != 0
        for q in range(19):
            adjoint_ref[q, x, rows, :] = jnp.where(is_fluid, through[q], turned[q])

    arrive(slow_2["middle"])
    send_middle(3, slow_3, third)
    sweep_interior(final)
    arrive(seed_rims)
    sweep(0, nx, lambda x: unpack_plane(4, held, x))
    unpack_corners(4, held, SLOW)
    unpack_corners(4, held, FAST)
    take_rows(3, post_3, slow_3, fast_3)
    sweep_edges(final)
    take_fast(3, post_3, fast_3)
    arrive(seed_faces[FAST])
    for y in range(tiles):
        final(face[FAST], y)
    take_outer(3, post_3, slow_3)
    arrive(slow_3["middle"])
    arrive(seed_faces[SLOW])
    for y in range(tiles):
        final(face[SLOW], y)
    for copy in sent:
        copy.wait_send()


def write_kernel(state_in, adjoint_in, state_ref, adjoint_ref, sem):
    made = []
    for i, (source, target) in enumerate(((state_in, state_ref), (adjoint_in, adjoint_ref))):
        for q in range(source.shape[0]):
            made.append(pltpu.make_async_copy(source.at[q], target.at[q], sem.at[i, q]))
    for copy in made:
        copy.start()
    for copy in made:
        copy.wait()


def per_device(checkpoint, fluid, adjoint_in):
    n, nx, ny, nz = checkpoint.shape
    padded = (n, nx + 2, ny + 2 * PAD, nz)
    f32 = jnp.float32
    state, adjoint = pl.pallas_call(
        forward_kernel,
        out_shape=(
            pltpu.VMEM((n, nx, ny, nz), f32),
            pltpu.VMEM((n, nx, ny, nz), f32),
        ),
        in_specs=[pl.BlockSpec(memory_space=pltpu.HBM)] * 3,
        out_specs=[pl.BlockSpec(memory_space=pltpu.VMEM)] * 2,
        scratch_shapes=[
            pltpu.VMEM(padded, f32),
            pltpu.VMEM(padded, f32),
            pltpu.VMEM(padded, f32),
            pltpu.VMEM(padded, f32),
            pltpu.VMEM((nx, ny, nz), jnp.int32),
            pltpu.VMEM((n, nx, ny, nz), f32),
            pltpu.VMEM((nx, ny, nz), jnp.int32),
            pltpu.VMEM(padded[1:], f32),
            pltpu.VMEM((5, 2, nx, 5, 1, nz), f32),
            pltpu.VMEM((5, 2, nx, 5, 1, nz), f32),
            pltpu.VMEM((5, 4, 1, nz), f32),
            pltpu.VMEM((5, 4, 1, nz), f32),
            pltpu.SemaphoreType.DMA((23,)),
            pltpu.SemaphoreType.DMA((5, LANES)),
            pltpu.SemaphoreType.DMA((5, LANES)),
            pltpu.SemaphoreType.DMA((2, 5)),
            pltpu.SemaphoreType.DMA((2, 5)),
        ],
        compiler_params=pltpu.CompilerParams(
            collective_id=0, has_side_effects=True, vmem_limit_bytes=50 * MIB
        ),
        name="forward",
    )(checkpoint, fluid, adjoint_in)
    return pl.pallas_call(
        write_kernel,
        out_shape=(jax.ShapeDtypeStruct((n, nx, ny, nz), f32),) * 2,
        in_specs=[pl.BlockSpec(memory_space=pltpu.VMEM)] * 2,
        out_specs=[pl.BlockSpec(memory_space=pl.ANY)] * 2,
        scratch_shapes=[pltpu.SemaphoreType.DMA((2, n))],
        compiler_params=pltpu.CompilerParams(vmem_limit_bytes=4 * MIB),
        name="write",
    )(state, adjoint)


def solution(mesh):
    return jax.shard_map(
        per_device,
        mesh=mesh,
        in_specs=(P(None, "gx", "gy", None), P("gx", "gy", None), P(None, "gx", "gy", None)),
        out_specs=(P(None, "gx", "gy", None), P(None, "gx", "gy", None)),
        check_vma=False,
    )
```

time: 33.8 us -> 31.9 us (0.944)
  Pallas kernels: 33 us -> 31.1 us
    pallas_call x1, Pallas kernels: 29 us -> 27.1 us  [per_device(): pl.pallas_call(forward_kernel, out_shape=(pltpu.VMEM((n, nx, ny, nz), f32...]
where the time goes in v1:
time: 31.9 us; the launch traced here: 31.8 us
  Pallas kernels  31.1 us (97%)
  between operations  0.64 us (2%)
    pallas_call x1, Pallas kernels, per_device(): pl.pallas_call(forward_kernel, out_shape=(pltpu.VMEM((n, nx, ny, nz), f32...  27.1 us
    pallas_call x1, Pallas kernels, per_device(): pl.pallas_call(write_kernel, out_shape=(jax.ShapeDtypeStruct((n, nx, ny,...  4.07 us

profile of v1, /device:TPU:0, one launch (start us, length us, event | category | flops | bytes accessed | tf_op | source)
XLA Modules:
  0.0 31.8 jit_solution(4589114489080810582)
XLA Ops:
  0.6 27.1 %forward.1 = (f32[19,8,64,128]{3,2,1,0:T(8,128)S(1)}, f32[19,8,64,128]{3,2,1,0:T(8,128)S(1)}) custom-call(f32[19,8,64,128]{3,2,1,0:T(8,128)} %start_ref.1, s32[8,64,128]{2,1,0:T(8,128)} %fluid_ref.1, f32[19,8,64,128]{3,2,1,0:T(8,128)} %seed_ref.1), custom_call_target="tpu_custom_call" | custom-call | tf_op jit(solution)/shard_map/forward/pallas_call | solution.py:551
  27.7 4.1 %write.1 = (f32[19,8,64,128]{3,2,1,0:T(8,128)}, f32[19,8,64,128]{3,2,1,0:T(8,128)}) custom-call(f32[19,8,64,128]{3,2,1,0:T(8,128)S(1)} %get-tuple-element.4.state_in, f32[19,8,64,128]{3,2,1,0:T(8,128)S(1)} %get-tuple-element.5.adjoint_in), custom_call_target="tpu_custom_call" | custom-call | tf_op jit(solution)/shard_map/write/pallas_call | solution.py:583

commit v2 on v1

--- a/solution.py
+++ b/solution.py
@@ -140,16 +140,17 @@
 
 
 SLOW, FAST = 0, 1
-LOW, HIGH, MIDDLE, OTHER, Y_SLOW, Y_REST, DIAGONAL = 0, 1, 2, 3, 4, 6, 8
-LANES = 12
+OUTER, MIDDLE, OTHER, ROWS = 0, 1, 2, 3
+CELLS_IN, SEEDS_IN, SEED_FACES_IN = 12, 13, 14
+CELLS_OUT, SLOW_OUT, REST_OUT = 0, 1, 2
 
 
 def forward_kernel(
     start_ref, fluid_ref, seed_ref,
     state_ref, adjoint_ref,
     post_1, post_2, post_3, held, bits_ref, start, cells, solid,
-    y_send, y_recv, c_send, c_recv,
-    load_sem, send_sem, recv_sem, seed_send, seed_recv,
+    y_send, y_recv,
+    load_sem, send_sem, recv_sem,
 ):
     _, nx, ny, nz = start_ref.shape
     tiles = ny // T
@@ -196,54 +197,66 @@
         pltpu.make_async_copy(
             seed_ref.at[q],
             held.at[SLOT[OPPOSITE[q]], pl.ds(1, nx), pl.ds(PAD, ny)],
-            load_sem.at[4 + q],
+            load_sem.at[4],
         )
         for q in range(19)
     ]
 
-    def remote(source, target, send, receive, to):
+    def wait_rows(rows, sem):
+        part = next(c for c in range(ny + 2 * PAD, 0, -T) if rows % c == 0)
+        outer = rows // part
+        planes = next(c for c in range(nx + 2, 0, -1) if outer % c == 0)
+        view = post_1.at[pl.ds(0, outer // planes), pl.ds(0, planes), pl.ds(0, part)]
+        pltpu.make_async_copy(view, view, sem).wait()
+
+    def remote(source, target, out, into, to):
         return pltpu.make_async_remote_copy(
-            src_ref=source, dst_ref=target, send_sem=send, recv_sem=receive,
+            src_ref=source, dst_ref=target, send_sem=send_sem.at[out], recv_sem=recv_sem.at[into],
             device_id=to, device_id_type=pl.DeviceIdType.MESH,
         )
+
+    def lane(e, kind):
+        return 4 * (e - 1) + kind
 
     seed_faces = {
         side: [
             remote(
                 seed_ref.at[2 * k + 5 + p if k else 1 + p, face[side]],
                 held.at[first_of(p) + k, halo_of(p), pl.ds(PAD, ny)],
-                seed_send.at[side, k], seed_recv.at[side, k], toward(side, 0),
+                SLOW_OUT if side == SLOW else REST_OUT,
+                SEED_FACES_IN if side == SLOW else SEEDS_IN,
+                toward(side, 0),
             )
             for k in range(5)
         ]
         for side, p in sign.items()
     }
 
-    def face_copy(e, lane, ref, side, first_tile, end_tile):
+    def face_copy(into, ref, side, first_tile, end_tile):
         p = sign[side]
         five, rows = pl.ds(first_of(p), 5), pl.ds(PAD + T * first_tile, T * (end_tile - first_tile))
         return remote(
             ref.at[five, face[side] + 1, rows], ref.at[five, halo_of(p), rows],
-            send_sem.at[e, lane], recv_sem.at[e, lane], toward(side, 0),
+            SLOW_OUT if side == SLOW else REST_OUT, into, toward(side, 0),
         )
 
-    def row_copies(e, lane, planes):
+    def row_copies(e, into, planes):
+        return [
+            remote(y_send.at[e, i, planes], y_recv.at[e, i, planes], REST_OUT, into, device(0, 1 - 2 * i))
+            for i in range(2)
+        ]
+
+    ends = ((pl.ds(top - T, T), pl.ds(PAD - T, T)), (pl.ds(PAD, T), pl.ds(top, T)))
+
+    def corner_copies(into, ref, side):
+        p = sign[side]
         return [
             remote(
-                y_send.at[e, i, planes], y_recv.at[e, i, planes],
-                send_sem.at[e, lane + i], recv_sem.at[e, lane + i], device(0, 1 - 2 * i),
+                ref.at[corner_of(p, i == 0), face[side] + 1, source],
+                ref.at[corner_of(p, i == 0), halo_of(p), target],
+                REST_OUT, into, toward(side, 1 - 2 * i),
             )
-            for i in range(2)
-        ]
-
-    def corner_copies(e, side):
-        return [
-            remote(
-                c_send.at[e, 2 * side + i], c_recv.at[e, 2 * side + i],
-                send_sem.at[e, DIAGONAL + 2 * side + i], recv_sem.at[e, DIAGONAL + 2 * side + i],
-                toward(side, 1 - 2 * i),
-            )
-            for i in range(2)
+            for i, (source, target) in enumerate(ends)
         ]
 
     def pack_plane(e, ref, x):
@@ -263,26 +276,9 @@
 
         lax.fori_loop(0, length, one, 0)
 
-    def pack_corners(e, ref, side):
-        p = sign[side]
-        c_send[e, 2 * side] = ref[corner_of(p, True), face[side] + 1, top - 1 : top, :]
-        c_send[e, 2 * side + 1] = ref[corner_of(p, False), face[side] + 1, PAD : PAD + 1, :]
-
-    def unpack_corners(e, ref, side):
-        p = 1 - sign[side]
-        ref[corner_of(p, True), halo_of(p), PAD - 1 : PAD, :] = c_recv[e, 2 * side]
-        ref[corner_of(p, False), halo_of(p), top : top + 1, :] = c_recv[e, 2 * side + 1]
-
-    sent = []
-
     def begin(made):
         for copy in made:
             copy.start()
-        sent.extend(made)
-
-    def arrive(made):
-        for copy in made:
-            copy.wait_recv()
 
     fluid_load.wait()
 
@@ -292,25 +288,20 @@
         y_send[0, 1, x, 0] = solid[x + 1, PAD : PAD + 1, :]
 
     sweep(0, nx, to_float)
-    for side in (SLOW, FAST):
-        c_send[0, 2 * side] = solid[face[side] + 1, top - 1 : top, :]
-        c_send[0, 2 * side + 1] = solid[face[side] + 1, PAD : PAD + 1, :]
     pl.semaphore_wait(barrier, len(around))
     cell_copies = [
         remote(
-            solid.at[face[side] + 1, pl.ds(PAD, ny)], solid.at[halo_of(sign[side]), pl.ds(PAD, ny)],
-            send_sem.at[0, side], recv_sem.at[0, side], toward(side, 0),
+            solid.at[face[side] + 1, source], solid.at[halo_of(sign[side]), target],
+            CELLS_OUT, CELLS_IN, toward(side, dy),
         )
         for side in (SLOW, FAST)
+        for dy, (source, target) in zip((0, 1, -1), ((pl.ds(PAD, ny),) * 2,) + ends)
     ]
-    for i in range(2):
-        cell_copies.append(
-            remote(
-                y_send.at[0, i, :, 0], y_recv.at[0, i, :, 0],
-                send_sem.at[0, Y_SLOW + i], recv_sem.at[0, Y_SLOW + i], device(0, 1 - 2 * i),
-            )
-        )
-    cell_copies += corner_copies(0, SLOW) + corner_copies(0, FAST)
+    cell_copies += [
+        remote(y_send.at[0, i, :, 0], y_recv.at[0, i, :, 0], CELLS_OUT, CELLS_IN, device(0, 1 - 2 * i))
+        for i in range(2)
+    ]
+    cell_rows = 2 * (ny + 2 * T + nx)
     begin(cell_copies)
 
     def store(to, x, y, v, is_fluid):
@@ -351,79 +342,59 @@
     def sweep_interior(body):
         sweep(1, nx - 2, inner_line(body))
 
-    def slow_copies(e, ref):
+    def send_outer(e, to, body):
         outer = 4 - e
-        return {
-            "outer": [
-                face_copy(e, LOW, ref, SLOW, 0, outer),
-                face_copy(e, HIGH, ref, SLOW, tiles - outer, tiles),
-            ],
-            "middle": [face_copy(e, MIDDLE, ref, SLOW, outer, tiles - outer)],
-            "corners": corner_copies(e, SLOW),
-            "rows": row_copies(e, Y_SLOW, pl.ds(face[SLOW], 1)),
-        }
-
-    def send_outer(e, to, body):
-        made = slow_copies(e, to)
-        outer = 4 - e
+        into = lane(e, OUTER)
         for i in range(outer):
             body(face[SLOW], i)
             body(face[SLOW], last - i)
             if i == 0:
-                pack_corners(e, to, SLOW)
+                begin(corner_copies(into, to, SLOW))
                 pack_plane(e, to, face[SLOW])
-                begin(made["corners"] + made["rows"])
-        begin(made["outer"])
-        return made
-
-    def send_middle(e, made, body):
+                begin(row_copies(e, lane(e, ROWS), pl.ds(face[SLOW], 1)))
+        begin([face_copy(into, to, SLOW, 0, outer), face_copy(into, to, SLOW, tiles - outer, tiles)])
+
+    def take_outer(e):
+        wait_rows(2 * T * (5 * (4 - e) + 1), recv_sem.at[lane(e, OUTER)])
+
+    def send_middle(e, to, body):
         outer = 4 - e
         for y in range(outer, tiles - outer):
             body(face[SLOW], y)
-        begin(made["middle"])
-
-    def other_copies(e, ref):
-        return {
-            "face": [face_copy(e, OTHER, ref, FAST, 0, tiles)] + corner_copies(e, FAST),
-            "rows": row_copies(e, Y_REST, rest),
-        }
+        begin([face_copy(lane(e, MIDDLE), to, SLOW, outer, tiles - outer)])
+
+    def take_middle(e):
+        wait_rows(5 * T * (tiles - 2 * (4 - e)), recv_sem.at[lane(e, MIDDLE)])
 
     def send_fast(e, to, body):
-        made = other_copies(e, to)
         for y in range(tiles):
             body(face[FAST], y)
-        pack_corners(e, to, FAST)
-        begin(made["face"])
-        return made
-
-    def send_rows(e, to, made):
+        into = lane(e, OTHER)
+        begin(corner_copies(into, to, FAST))
+        begin([face_copy(into, to, FAST, 0, tiles)])
+
+    def take_fast(e):
+        wait_rows(5 * ny + 2 * T, recv_sem.at[lane(e, OTHER)])
+
+    def send_rows(e, to):
         sweep(1 - odd, nx - 1, lambda x: pack_plane(e, to, x))
-        begin(made["rows"])
-
-    def take_rows(e, ref, slow, other):
-        arrive(slow["rows"] + other["rows"])
+        begin(row_copies(e, lane(e, ROWS), rest))
+
+    def take_rows(e, ref):
+        wait_rows(10 * nx, recv_sem.at[lane(e, ROWS)])
         sweep(0, nx, lambda x: unpack_plane(e, ref, x))
 
-    def take_fast(e, ref, made):
-        arrive(made["face"])
-        unpack_corners(e, ref, FAST)
-
-    def take_outer(e, ref, made):
-        arrive(made["corners"])
-        unpack_corners(e, ref, SLOW)
-        arrive(made["outer"])
-
     start_load[0].wait()
-    slow_1 = send_outer(1, post_1, first)
-    send_middle(1, slow_1, first)
+    send_outer(1, post_1, first)
+    send_middle(1, post_1, first)
     begin(seed_faces[SLOW][:2])
     start_load[1].wait()
-    fast_1 = send_fast(1, post_1, first)
+    send_fast(1, post_1, first)
     start_load[2].wait()
     for load in seed_load:
         load.start()
     sweep_edges(first)
-    send_rows(1, post_1, fast_1)
+    send_rows(1, post_1)
     sweep_interior(first)
 
     layer = lax.broadcasted_iota(jnp.int32, (T, nz), 1)
@@ -449,26 +420,19 @@
     second = middle(post_1, post_2)
     sweep_interior(second)
 
-    for load in seed_load:
-        load.wait()
+    wait_rows(19 * nx * ny, load_sem.at[4])
     sweep(0, nx, lambda x: pack_plane(4, held, x))
-    pack_corners(4, held, SLOW)
-    pack_corners(4, held, FAST)
-    seed_rims = row_copies(4, Y_SLOW, pl.ds(0, nx)) + corner_copies(4, SLOW) + corner_copies(4, FAST)
-    begin(seed_rims)
+    begin(row_copies(4, SEEDS_IN, pl.ds(0, nx)))
+    begin(corner_copies(SEEDS_IN, held, SLOW) + corner_copies(SEEDS_IN, held, FAST))
     begin(seed_faces[FAST])
 
-    arrive(cell_copies)
+    wait_rows(cell_rows, recv_sem.at[CELLS_IN])
 
     def place_cells(x):
         solid[x + 1, PAD - 1 : PAD, :] = y_recv[0, 0, x, 0]
         solid[x + 1, top : top + 1, :] = y_recv[0, 1, x, 0]
 
     sweep(0, nx, place_cells)
-    for side in (SLOW, FAST):
-        halo = halo_of(1 - sign[side])
-        solid[halo, PAD - 1 : PAD, :] = c_recv[0, 2 * side]
-        solid[halo, top : top + 1, :] = c_recv[0, 2 * side + 1]
     sweep_edges(mark)
 
     def mark_face(i):
@@ -477,26 +441,26 @@
 
     sweep(0, 2, mark_face)
 
-    take_rows(1, post_1, slow_1, fast_1)
+    take_rows(1, post_1)
     sweep_edges(second)
-    take_fast(1, post_1, fast_1)
-    fast_2 = send_fast(2, post_2, second)
-    send_rows(2, post_2, fast_2)
-    take_outer(1, post_1, slow_1)
-    slow_2 = send_outer(2, post_2, second)
-    arrive(slow_1["middle"])
-    send_middle(2, slow_2, second)
+    take_fast(1)
+    send_fast(2, post_2, second)
+    send_rows(2, post_2)
+    take_outer(1)
+    send_outer(2, post_2, second)
+    take_middle(1)
+    send_middle(2, post_2, second)
     begin(seed_faces[SLOW][2:4])
 
     third = middle(post_2, post_3)
     sweep_interior(third)
-    take_rows(2, post_2, slow_2, fast_2)
+    take_rows(2, post_2)
     sweep_edges(third)
-    take_fast(2, post_2, fast_2)
-    fast_3 = send_fast(3, post_3, third)
-    send_rows(3, post_3, fast_3)
-    take_outer(2, post_2, slow_2)
-    slow_3 = send_outer(3, post_3, third)
+    take_fast(2)
+    send_fast(3, post_3, third)
+    send_rows(3, post_3)
+    take_outer(2)
+    send_outer(3, post_3, third)
     begin(seed_faces[SLOW][4:])
 
     def final(x, y):
@@ -511,33 +475,29 @@
         for q in range(19):
             adjoint_ref[q, x, rows, :] = jnp.where(is_fluid, through[q], turned[q])
 
-    arrive(slow_2["middle"])
-    send_middle(3, slow_3, third)
+    take_middle(2)
+    send_middle(3, post_3, third)
     sweep_interior(final)
-    arrive(seed_rims)
+    wait_rows(5 * ny + 10 * nx + 4 * T, recv_sem.at[SEEDS_IN])
     sweep(0, nx, lambda x: unpack_plane(4, held, x))
-    unpack_corners(4, held, SLOW)
-    unpack_corners(4, held, FAST)
-    take_rows(3, post_3, slow_3, fast_3)
+    take_rows(3, post_3)
     sweep_edges(final)
-    take_fast(3, post_3, fast_3)
-    arrive(seed_faces[FAST])
+    take_fast(3)
     for y in range(tiles):
         final(face[FAST], y)
-    take_outer(3, post_3, slow_3)
-    arrive(slow_3["middle"])
-    arrive(seed_faces[SLOW])
+    take_outer(3)
+    take_middle(3)
+    wait_rows(5 * ny, recv_sem.at[SEED_FACES_IN])
     for y in range(tiles):
         final(face[SLOW], y)
-    for copy in sent:
-        copy.wait_send()
+    wait_rows(cell_rows, send_sem.at[CELLS_OUT])
+    wait_rows(4 * 5 * ny, send_sem.at[SLOW_OUT])
+    wait_rows(4 * (5 * ny + 10 * nx + 4 * T), send_sem.at[REST_OUT])
 
 
 def write_kernel(state_in, adjoint_in, state_ref, adjoint_ref, sem):
-    made = []
-    for i, (source, target) in enumerate(((state_in, state_ref), (adjoint_in, adjoint_ref))):
-        for q in range(source.shape[0]):
-            made.append(pltpu.make_async_copy(source.at[q], target.at[q], sem.at[i, q]))
+    pairs = ((state_in, state_ref), (adjoint_in, adjoint_ref))
+    made = [pltpu.make_async_copy(source, target, sem.at[i]) for i, (source, target) in enumerate(pairs)]
     for copy in made:
         copy.start()
     for copy in made:
@@ -567,13 +527,9 @@
             pltpu.VMEM(padded[1:], f32),
             pltpu.VMEM((5, 2, nx, 5, 1, nz), f32),
             pltpu.VMEM((5, 2, nx, 5, 1, nz), f32),
-            pltpu.VMEM((5, 4, 1, nz), f32),
-            pltpu.VMEM((5, 4, 1, nz), f32),
-            pltpu.SemaphoreType.DMA((23,)),
-            pltpu.SemaphoreType.DMA((5, LANES)),
-            pltpu.SemaphoreType.DMA((5, LANES)),
-            pltpu.SemaphoreType.DMA((2, 5)),
-            pltpu.SemaphoreType.DMA((2, 5)),
+            pltpu.SemaphoreType.DMA((5,)),
+            pltpu.SemaphoreType.DMA((3,)),
+            pltpu.SemaphoreType.DMA((15,)),
         ],
         compiler_params=pltpu.CompilerParams(
             collective_id=0, has_side_effects=True, vmem_limit_bytes=50 * MIB
@@ -585,7 +541,7 @@
         out_shape=(jax.ShapeDtypeStruct((n, nx, ny, nz), f32),) * 2,
         in_specs=[pl.BlockSpec(memory_space=pltpu.VMEM)] * 2,
         out_specs=[pl.BlockSpec(memory_space=pl.ANY)] * 2,
-        scratch_shapes=[pltpu.SemaphoreType.DMA((2, n))],
+        scratch_shapes=[pltpu.SemaphoreType.DMA((2,))],
         compiler_params=pltpu.CompilerParams(vmem_limit_bytes=4 * MIB),
         name="write",
     )(state, adjoint)

time: 31.9 us -> 30.4 us (0.953)
  Pallas kernels: 31.1 us -> 29.6 us
    pallas_call x1, Pallas kernels: 27.1 us -> 25.7 us  [per_device(): pl.pallas_call(forward_kernel, out_shape=(pltpu.VMEM((n, nx, ny, nz), f32...]
where the time goes in v2:
time: 30.4 us; the launch traced here: 30.3 us
  Pallas kernels  29.6 us (97%)
  between operations  0.64 us (2%)
    pallas_call x1, Pallas kernels, per_device(): pl.pallas_call(forward_kernel, out_shape=(pltpu.VMEM((n, nx, ny, nz), f32...  25.7 us
    pallas_call x1, Pallas kernels, per_device(): pl.pallas_call(write_kernel, out_shape=(jax.ShapeDtypeStruct((n, nx, ny,...  3.93 us

profile of v2, /device:TPU:0, one launch (start us, length us, event | category | flops | bytes accessed | tf_op | source)
XLA Modules:
  0.0 30.3 jit_solution(8582351600064543247)
XLA Ops:
  0.6 25.7 %forward.1 = (f32[19,8,64,128]{3,2,1,0:T(8,128)S(1)}, f32[19,8,64,128]{3,2,1,0:T(8,128)S(1)}) custom-call(f32[19,8,64,128]{3,2,1,0:T(8,128)} %start_ref.1, s32[8,64,128]{2,1,0:T(8,128)} %fluid_ref.1, f32[19,8,64,128]{3,2,1,0:T(8,128)} %seed_ref.1), custom_call_target="tpu_custom_call" | custom-call | tf_op jit(solution)/shard_map/forward/pallas_call | solution.py:511
  26.3 3.9 %write.1 = (f32[19,8,64,128]{3,2,1,0:T(8,128)}, f32[19,8,64,128]{3,2,1,0:T(8,128)}) custom-call(f32[19,8,64,128]{3,2,1,0:T(8,128)S(1)} %get-tuple-element.4.state_in, f32[19,8,64,128]{3,2,1,0:T(8,128)S(1)} %get-tuple-element.5.adjoint_in), custom_call_target="tpu_custom_call" | custom-call | tf_op jit(solution)/shard_map/write/pallas_call | solution.py:539

commit v3 on v2

--- a/solution.py
+++ b/solution.py
@@ -187,9 +187,17 @@
 
     fluid_load = pltpu.make_async_copy(fluid_ref, cells, load_sem.at[0])
     fluid_load.start()
+    slow_plane, fast_plane = pl.ds(face[SLOW], 1), pl.ds(face[FAST], 1)
+    inner = pl.ds(1, nx - 2)
     start_load = [
-        pltpu.make_async_copy(start_ref.at[:, planes], start.at[:, planes], load_sem.at[1 + i])
-        for i, planes in enumerate((pl.ds(face[SLOW], 1), pl.ds(face[FAST], 1), pl.ds(1, nx - 2)))
+        pltpu.make_async_copy(start_ref.at[:, planes, rows], start.at[:, planes, rows], load_sem.at[i])
+        for i, planes, rows in (
+            (1, slow_plane, pl.ds(0, ny)),
+            (2, inner, pl.ds(0, T)),
+            (2, inner, pl.ds(ny - T, T)),
+            (2, fast_plane, pl.ds(0, ny)),
+            (3, inner, pl.ds(T, ny - 2 * T)),
+        )
     ]
     for load in start_load:
         load.start()
@@ -203,10 +211,13 @@
     ]
 
     def wait_rows(rows, sem):
-        part = next(c for c in range(ny + 2 * PAD, 0, -T) if rows % c == 0)
-        outer = rows // part
-        planes = next(c for c in range(nx + 2, 0, -1) if outer % c == 0)
-        view = post_1.at[pl.ds(0, outer // planes), pl.ds(0, planes), pl.ds(0, part)]
+        part, planes = next(
+            (c, d)
+            for c in range(ny + 2 * PAD, 0, -T)
+            for d in range(nx + 2, 0, -1)
+            if rows % (c * d) == 0 and rows <= 19 * c * d
+        )
+        view = post_1.at[pl.ds(0, rows // (part * planes)), pl.ds(0, planes), pl.ds(0, part)]
         pltpu.make_async_copy(view, view, sem).wait()
 
     def remote(source, target, out, into, to):
@@ -269,12 +280,12 @@
             ref[SLOT[UP[k]], x + 1, PAD - 1 : PAD, :] = y_recv[e, 0, x, k]
             ref[SLOT[DOWN[k]], x + 1, top : top + 1, :] = y_recv[e, 1, x, k]
 
-    def sweep(begin_at, length, body):
+    def sweep(begin_at, length, body, unroll=True):
         def one(i, _):
             body(begin_at + i)
             return 0
 
-        lax.fori_loop(0, length, one, 0)
+        lax.fori_loop(0, length, one, 0, unroll=unroll)
 
     def begin(made):
         for copy in made:
@@ -337,10 +348,10 @@
         return line
 
     def sweep_edges(body):
-        sweep(1, nx - 2, edge_line(body))
+        sweep(1 - odd, nx - 1, edge_line(body))
 
     def sweep_interior(body):
-        sweep(1, nx - 2, inner_line(body))
+        sweep(1, nx - 2, inner_line(body), 1)
 
     def send_outer(e, to, body):
         outer = 4 - e
@@ -366,19 +377,19 @@
     def take_middle(e):
         wait_rows(5 * T * (tiles - 2 * (4 - e)), recv_sem.at[lane(e, MIDDLE)])
 
+    def send_edges(e, to, body):
+        sweep_edges(body)
+        begin(corner_copies(lane(e, OTHER), to, FAST))
+        sweep(1 - odd, nx - 1, lambda x: pack_plane(e, to, x))
+        begin(row_copies(e, lane(e, ROWS), rest))
+
     def send_fast(e, to, body):
-        for y in range(tiles):
+        for y in range(1, last):
             body(face[FAST], y)
-        into = lane(e, OTHER)
-        begin(corner_copies(into, to, FAST))
-        begin([face_copy(into, to, FAST, 0, tiles)])
+        begin([face_copy(lane(e, OTHER), to, FAST, 0, tiles)])
 
     def take_fast(e):
         wait_rows(5 * ny + 2 * T, recv_sem.at[lane(e, OTHER)])
-
-    def send_rows(e, to):
-        sweep(1 - odd, nx - 1, lambda x: pack_plane(e, to, x))
-        begin(row_copies(e, lane(e, ROWS), rest))
 
     def take_rows(e, ref):
         wait_rows(10 * nx, recv_sem.at[lane(e, ROWS)])
@@ -387,14 +398,13 @@
     start_load[0].wait()
     send_outer(1, post_1, first)
     send_middle(1, post_1, first)
-    begin(seed_faces[SLOW][:2])
-    start_load[1].wait()
+    begin(seed_faces[SLOW][:3])
+    wait_rows(19 * (2 * T * (nx - 2) + ny), load_sem.at[2])
+    send_edges(1, post_1, first)
     send_fast(1, post_1, first)
-    start_load[2].wait()
+    wait_rows(19 * (nx - 2) * (ny - 2 * T), load_sem.at[3])
     for load in seed_load:
         load.start()
-    sweep_edges(first)
-    send_rows(1, post_1)
     sweep_interior(first)
 
     layer = lax.broadcasted_iota(jnp.int32, (T, nz), 1)
@@ -433,32 +443,25 @@
         solid[x + 1, top : top + 1, :] = y_recv[0, 1, x, 0]
 
     sweep(0, nx, place_cells)
-    sweep_edges(mark)
-
-    def mark_face(i):
-        for y in range(tiles):
-            mark(i * (nx - 1), y)
-
-    sweep(0, 2, mark_face)
+    sweep(0, nx, edge_line(mark))
+    sweep(0, 2, lambda i: inner_line(mark)(i * (nx - 1)))
 
     take_rows(1, post_1)
-    sweep_edges(second)
     take_fast(1)
+    send_edges(2, post_2, second)
     send_fast(2, post_2, second)
-    send_rows(2, post_2)
     take_outer(1)
     send_outer(2, post_2, second)
     take_middle(1)
     send_middle(2, post_2, second)
-    begin(seed_faces[SLOW][2:4])
+    begin(seed_faces[SLOW][3:4])
 
     third = middle(post_2, post_3)
     sweep_interior(third)
     take_rows(2, post_2)
-    sweep_edges(third)
     take_fast(2)
+    send_edges(3, post_3, third)
     send_fast(3, post_3, third)
-    send_rows(3, post_3)
     take_outer(2)
     send_outer(3, post_3, third)
     begin(seed_faces[SLOW][4:])
@@ -481,9 +484,9 @@
     wait_rows(5 * ny + 10 * nx + 4 * T, recv_sem.at[SEEDS_IN])
     sweep(0, nx, lambda x: unpack_plane(4, held, x))
     take_rows(3, post_3)
+    take_fast(3)
     sweep_edges(final)
-    take_fast(3)
-    for y in range(tiles):
+    for y in range(1, last):
         final(face[FAST], y)
     take_outer(3)
     take_middle(3)
@@ -497,11 +500,11 @@
 
 def write_kernel(state_in, adjoint_in, state_ref, adjoint_ref, sem):
     pairs = ((state_in, state_ref), (adjoint_in, adjoint_ref))
-    made = [pltpu.make_async_copy(source, target, sem.at[i]) for i, (source, target) in enumerate(pairs)]
-    for copy in made:
-        copy.start()
-    for copy in made:
-        copy.wait()
+    for i, (source, target) in enumerate(pairs):
+        for q in range(source.shape[0]):
+            pltpu.make_async_copy(source.at[q], target.at[q], sem.at[i]).start()
+    for i, (source, target) in enumerate(pairs):
+        pltpu.make_async_copy(source, target, sem.at[i]).wait()
 
 
 def per_device(checkpoint, fluid, adjoint_in):

time: 30.4 us -> 29.8 us (0.980)
  Pallas kernels: 29.6 us -> 29 us
    pallas_call x1, Pallas kernels: 25.7 us -> 25.3 us  [per_device(): pl.pallas_call(forward_kernel, out_shape=(pltpu.VMEM((n, nx, ny, nz), f32...]
where the time goes in v3:
time: 29.8 us; the launch traced here: 29.7 us
  Pallas kernels  29 us (97%)
  between operations  0.64 us (2%)
    pallas_call x1, Pallas kernels, per_device(): pl.pallas_call(forward_kernel, out_shape=(pltpu.VMEM((n, nx, ny, nz), f32...  25.3 us
    pallas_call x1, Pallas kernels, per_device(): pl.pallas_call(write_kernel, out_shape=(jax.ShapeDtypeStruct((n, nx, ny,...  3.74 us

profile of v3, /device:TPU:0, one launch (start us, length us, event | category | flops | bytes accessed | tf_op | source)
XLA Modules:
  0.0 29.7 jit_solution(234180771693787131)
XLA Ops:
  0.6 25.3 %forward.1 = (f32[19,8,64,128]{3,2,1,0:T(8,128)S(1)}, f32[19,8,64,128]{3,2,1,0:T(8,128)S(1)}) custom-call(f32[19,8,64,128]{3,2,1,0:T(8,128)} %start_ref.1, s32[8,64,128]{2,1,0:T(8,128)} %fluid_ref.1, f32[19,8,64,128]{3,2,1,0:T(8,128)} %seed_ref.1), custom_call_target="tpu_custom_call" | custom-call | tf_op jit(solution)/shard_map/forward/pallas_call | solution.py:514
  25.9 3.7 %write.1 = (f32[19,8,64,128]{3,2,1,0:T(8,128)}, f32[19,8,64,128]{3,2,1,0:T(8,128)}) custom-call(f32[19,8,64,128]{3,2,1,0:T(8,128)S(1)} %get-tuple-element.4.state_in, f32[19,8,64,128]{3,2,1,0:T(8,128)S(1)} %get-tuple-element.5.adjoint_in), custom_call_target="tpu_custom_call" | custom-call | tf_op jit(solution)/shard_map/write/pallas_call | solution.py:542

commit v4 on v3

--- a/solution.py
+++ b/solution.py
@@ -291,6 +291,13 @@
         for copy in made:
             copy.start()
 
+    turn = lax.rem(me["gx"] + 1, 4)
+
+    def send_seeds(near):
+        @pl.when(turn >= 2 if near else turn < 2)
+        def _():
+            begin(seed_faces[SLOW])
+
     fluid_load.wait()
 
     def to_float(x):
@@ -398,7 +405,7 @@
     start_load[0].wait()
     send_outer(1, post_1, first)
     send_middle(1, post_1, first)
-    begin(seed_faces[SLOW][:3])
+    send_seeds(False)
     wait_rows(19 * (2 * T * (nx - 2) + ny), load_sem.at[2])
     send_edges(1, post_1, first)
     send_fast(1, post_1, first)
@@ -454,7 +461,6 @@
     send_outer(2, post_2, second)
     take_middle(1)
     send_middle(2, post_2, second)
-    begin(seed_faces[SLOW][3:4])
 
     third = middle(post_2, post_3)
     sweep_interior(third)
@@ -464,7 +470,7 @@
     send_fast(3, post_3, third)
     take_outer(2)
     send_outer(3, post_3, third)
-    begin(seed_faces[SLOW][4:])
+    send_seeds(True)
 
     def final(x, y):
         rows = slice(T * y, T * y + T)

time: 29.8 us -> 28.8 us (0.966)
  Pallas kernels: 29 us -> 28 us
    pallas_call x1, Pallas kernels: 25.3 us -> 24.3 us  [per_device(): pl.pallas_call(forward_kernel, out_shape=(pltpu.VMEM((n, nx, ny, nz), f32...]
where the time goes in v4:
time: 28.8 us; the launch traced here: 28.7 us
  Pallas kernels  28 us (97%)
  between operations  0.64 us (2%)
    pallas_call x1, Pallas kernels, per_device(): pl.pallas_call(forward_kernel, out_shape=(pltpu.VMEM((n, nx, ny, nz), f32...  24.3 us
    pallas_call x1, Pallas kernels, per_device(): pl.pallas_call(write_kernel, out_shape=(jax.ShapeDtypeStruct((n, nx, ny,...  3.74 us

profile of v4, /device:TPU:0, one launch (start us, length us, event | category | flops | bytes accessed | tf_op | source)
XLA Modules:
  0.0 28.7 jit_solution(15962801192457592085)
XLA Ops:
  0.6 24.3 %forward.1 = (f32[19,8,64,128]{3,2,1,0:T(8,128)S(1)}, f32[19,8,64,128]{3,2,1,0:T(8,128)S(1)}) custom-call(f32[19,8,64,128]{3,2,1,0:T(8,128)} %start_ref.1, s32[8,64,128]{2,1,0:T(8,128)} %fluid_ref.1, f32[19,8,64,128]{3,2,1,0:T(8,128)} %seed_ref.1), custom_call_target="tpu_custom_call" | custom-call | tf_op jit(solution)/shard_map/forward/pallas_call | solution.py:520
  24.9 3.7 %write.1 = (f32[19,8,64,128]{3,2,1,0:T(8,128)}, f32[19,8,64,128]{3,2,1,0:T(8,128)}) custom-call(f32[19,8,64,128]{3,2,1,0:T(8,128)S(1)} %get-tuple-element.4.state_in, f32[19,8,64,128]{3,2,1,0:T(8,128)S(1)} %get-tuple-element.5.adjoint_in), custom_call_target="tpu_custom_call" | custom-call | tf_op jit(solution)/shard_map/write/pallas_call | solution.py:548

commit v5 on v4

--- a/solution.py
+++ b/solution.py
@@ -139,6 +139,15 @@
     return result
 
 
+def last_step(post, held, bits_ref, x, y):
+    bits = bits_ref[x, T * y : T * y + T, :]
+    v = stream(post, bits, x, y)
+    turned = stream(held, bits, x, y)
+    through = pull_back(v, [turned[OPPOSITE[q]] for q in range(19)])
+    is_fluid = (bits & 1) != 0
+    return v, [jnp.where(is_fluid, through[q], turned[q]) for q in range(19)]
+
+
 SLOW, FAST = 0, 1
 OUTER, MIDDLE, OTHER, ROWS = 0, 1, 2, 3
 CELLS_IN, SEEDS_IN, SEED_FACES_IN = 12, 13, 14
@@ -147,8 +156,8 @@
 
 def forward_kernel(
     start_ref, fluid_ref, seed_ref,
-    state_ref, adjoint_ref,
-    post_1, post_2, post_3, held, bits_ref, start, cells, solid,
+    state_ref, adjoint_ref, post_3, held, bits_ref,
+    post_1, post_2, start, cells, solid,
     y_send, y_recv,
     load_sem, send_sem, recv_sem,
 ):
@@ -474,15 +483,10 @@
 
     def final(x, y):
         rows = slice(T * y, T * y + T)
-        bits = bits_ref[x, rows, :]
-        v = stream(post_3, bits, x, y)
+        v, through = last_step(post_3, held, bits_ref, x, y)
         for q in range(19):
             state_ref[q, x, rows, :] = v[q]
-        turned = stream(held, bits, x, y)
-        through = pull_back(v, [turned[OPPOSITE[q]] for q in range(19)])
-        is_fluid = (bits & 1) != 0
-        for q in range(19):
-            adjoint_ref[q, x, rows, :] = jnp.where(is_fluid, through[q], turned[q])
+            adjoint_ref[q, x, rows, :] = through[q]
 
     take_middle(2)
     send_middle(3, post_3, third)
@@ -497,40 +501,57 @@
     take_outer(3)
     take_middle(3)
     wait_rows(5 * ny, recv_sem.at[SEED_FACES_IN])
-    for y in range(tiles):
-        final(face[SLOW], y)
     wait_rows(cell_rows, send_sem.at[CELLS_OUT])
     wait_rows(4 * 5 * ny, send_sem.at[SLOW_OUT])
     wait_rows(4 * (5 * ny + 10 * nx + 4 * T), send_sem.at[REST_OUT])
 
 
-def write_kernel(state_in, adjoint_in, state_ref, adjoint_ref, sem):
-    pairs = ((state_in, state_ref), (adjoint_in, adjoint_ref))
-    for i, (source, target) in enumerate(pairs):
-        for q in range(source.shape[0]):
-            pltpu.make_async_copy(source.at[q], target.at[q], sem.at[i]).start()
-    for i, (source, target) in enumerate(pairs):
-        pltpu.make_async_copy(source, target, sem.at[i]).wait()
+def write_kernel(
+    state_in, adjoint_in, post, held, bits_ref, state_ref, adjoint_ref, state_face, adjoint_face, sem
+):
+    n, nx, ny, _ = state_in.shape
+    odd = lax.rem(lax.axis_index("gx"), 2)
+    slow = (nx - 1) * odd
+    triples = ((state_in, state_face, state_ref), (adjoint_in, adjoint_face, adjoint_ref))
+    rest = pl.ds(1 - odd, nx - 1)
+    for i, (source, _, target) in enumerate(triples):
+        for q in range(n):
+            pltpu.make_async_copy(source.at[q, rest], target.at[q, rest], sem.at[i]).start()
+    for y in range(ny // T):
+        v, through = last_step(post, held, bits_ref, slow, y)
+        for q in range(n):
+            state_face[q, T * y : T * y + T, :] = v[q]
+            adjoint_face[q, T * y : T * y + T, :] = through[q]
+    faces = [
+        pltpu.make_async_copy(source, target.at[:, slow], sem.at[2 + i])
+        for i, (_, source, target) in enumerate(triples)
+    ]
+    for copy in faces:
+        copy.start()
+    for i, (source, _, target) in enumerate(triples):
+        pltpu.make_async_copy(source.at[:, rest], target.at[:, rest], sem.at[i]).wait()
+    for copy in faces:
+        copy.wait()
 
 
 def per_device(checkpoint, fluid, adjoint_in):
     n, nx, ny, nz = checkpoint.shape
     padded = (n, nx + 2, ny + 2 * PAD, nz)
     f32 = jnp.float32
-    state, adjoint = pl.pallas_call(
+    results = pl.pallas_call(
         forward_kernel,
         out_shape=(
             pltpu.VMEM((n, nx, ny, nz), f32),
             pltpu.VMEM((n, nx, ny, nz), f32),
+            pltpu.VMEM(padded, f32),
+            pltpu.VMEM(padded, f32),
+            pltpu.VMEM((nx, ny, nz), jnp.int32),
         ),
         in_specs=[pl.BlockSpec(memory_space=pltpu.HBM)] * 3,
-        out_specs=[pl.BlockSpec(memory_space=pltpu.VMEM)] * 2,
+        out_specs=[pl.BlockSpec(memory_space=pltpu.VMEM)] * 5,
         scratch_shapes=[
             pltpu.VMEM(padded, f32),
             pltpu.VMEM(padded, f32),
-            pltpu.VMEM(padded, f32),
-            pltpu.VMEM(padded, f32),
-            pltpu.VMEM((nx, ny, nz), jnp.int32),
             pltpu.VMEM((n, nx, ny, nz), f32),
             pltpu.VMEM((nx, ny, nz), jnp.int32),
             pltpu.VMEM(padded[1:], f32),
@@ -541,19 +562,23 @@
             pltpu.SemaphoreType.DMA((15,)),
         ],
         compiler_params=pltpu.CompilerParams(
-            collective_id=0, has_side_effects=True, vmem_limit_bytes=50 * MIB
+            collective_id=0, has_side_effects=True, vmem_limit_bytes=30 * MIB
         ),
         name="forward",
     )(checkpoint, fluid, adjoint_in)
     return pl.pallas_call(
         write_kernel,
         out_shape=(jax.ShapeDtypeStruct((n, nx, ny, nz), f32),) * 2,
-        in_specs=[pl.BlockSpec(memory_space=pltpu.VMEM)] * 2,
+        in_specs=[pl.BlockSpec(memory_space=pltpu.VMEM)] * 5,
         out_specs=[pl.BlockSpec(memory_space=pl.ANY)] * 2,
-        scratch_shapes=[pltpu.SemaphoreType.DMA((2,))],
+        scratch_shapes=[
+            pltpu.VMEM((n, ny, nz), f32),
+            pltpu.VMEM((n, ny, nz), f32),
+            pltpu.SemaphoreType.DMA((4,)),
+        ],
         compiler_params=pltpu.CompilerParams(vmem_limit_bytes=4 * MIB),
         name="write",
-    )(state, adjoint)
+    )(*results)
 
 
 def solution(mesh):

time: 28.8 us -> 28.5 us (0.990)
  Pallas kernels: 28 us -> 27.7 us
    pallas_call x1, Pallas kernels: 24.3 us -> 23.9 us  [per_device(): pl.pallas_call(forward_kernel, out_shape=(pltpu.VMEM((n, nx, ny, nz), f32...]
where the time goes in v5:
time: 28.5 us; the launch traced here: 28.3 us
  Pallas kernels  27.7 us (97%)
  between operations  0.64 us (2%)
    pallas_call x1, Pallas kernels, per_device(): pl.pallas_call(forward_kernel, out_shape=(pltpu.VMEM((n, nx, ny, nz), f32...  23.9 us
    pallas_call x1, Pallas kernels, per_device(): pl.pallas_call(write_kernel, out_shape=(jax.ShapeDtypeStruct((n, nx, ny,...  3.81 us

profile of v5, /device:TPU:0, one launch (start us, length us, event | category | flops | bytes accessed | tf_op | source)
XLA Modules:
  0.0 28.3 jit_solution(2638238275370187601)
XLA Ops:
  0.6 23.9 %forward.1 = (f32[19,8,64,128]{3,2,1,0:T(8,128)S(1)}, f32[19,8,64,128]{3,2,1,0:T(8,128)S(1)}, f32[19,10,80,128]{3,2,1,0:T(8,128)S(1)}, f32[19,10,80,128]{3,2,1,0:T(8,128)S(1)}, s32[8,64,128]{2,1,0:T(8,128)S(1)}) custom-call(f32[19,8,64,128]{3,2,1,0:T(8,128)} %start_ref.1, s32[8,64,128]{2,1,0:T(8,128)} %fluid_ref.1, f32[19,8,64,128]{3,2,1,0:T(8,128)} %seed_ref.1), custom_call_target="tpu_custom_call" | custom-call | tf_op jit(solution)/shard_map/forward/pallas_call | solution.py:541
  24.5 3.8 %write.1 = (f32[19,8,64,128]{3,2,1,0:T(8,128)}, f32[19,8,64,128]{3,2,1,0:T(8,128)}) custom-call(f32[19,8,64,128]{3,2,1,0:T(8,128)S(1)} %get-tuple-element.7.state_in, f32[19,8,64,128]{3,2,1,0:T(8,128)S(1)} %get-tuple-element.8.adjoint_in, f32[19,10,80,128]{3,2,1,0:T(8,128)S(1)} %get-tuple-element.9.post, f32[19,10,80,128]{3,2,1,0:T(8,128)S(1)} %get-tuple-element.10.held, ...), custom_call_target="tpu_custom_call" | custom-call | tf_op jit(solution)/shard_map/write/pallas_call | solution.py:569

commit v6 on v5

--- a/solution.py
+++ b/solution.py
@@ -465,9 +465,9 @@
     take_rows(1, post_1)
     take_fast(1)
     send_edges(2, post_2, second)
-    send_fast(2, post_2, second)
     take_outer(1)
     send_outer(2, post_2, second)
+    send_fast(2, post_2, second)
     take_middle(1)
     send_middle(2, post_2, second)
 
@@ -476,9 +476,9 @@
     take_rows(2, post_2)
     take_fast(2)
     send_edges(3, post_3, third)
-    send_fast(3, post_3, third)
     take_outer(2)
     send_outer(3, post_3, third)
+    send_fast(3, post_3, third)
     send_seeds(True)
 
     def final(x, y):

time: 28.5 us -> 28.8 us (1.011)
  Pallas kernels: 27.7 us -> 28 us
where the time goes in v6:
time: 28.8 us; the launch traced here: 28.6 us
  Pallas kernels  28 us (97%)
  between operations  0.64 us (2%)
    pallas_call x1, Pallas kernels, per_device(): pl.pallas_call(forward_kernel, out_shape=(pltpu.VMEM((n, nx, ny, nz), f32...  24.2 us
    pallas_call x1, Pallas kernels, per_device(): pl.pallas_call(write_kernel, out_shape=(jax.ShapeDtypeStruct((n, nx, ny,...  3.81 us

profile of v6, /device:TPU:0, one launch (start us, length us, event | category | flops | bytes accessed | tf_op | source)
XLA Modules:
  0.0 28.6 jit_solution(5107597377049730422)
XLA Ops:
  0.6 24.2 %forward.1 = (f32[19,8,64,128]{3,2,1,0:T(8,128)S(1)}, f32[19,8,64,128]{3,2,1,0:T(8,128)S(1)}, f32[19,10,80,128]{3,2,1,0:T(8,128)S(1)}, f32[19,10,80,128]{3,2,1,0:T(8,128)S(1)}, s32[8,64,128]{2,1,0:T(8,128)S(1)}) custom-call(f32[19,8,64,128]{3,2,1,0:T(8,128)} %start_ref.1, s32[8,64,128]{2,1,0:T(8,128)} %fluid_ref.1, f32[19,8,64,128]{3,2,1,0:T(8,128)} %seed_ref.1), custom_call_target="tpu_custom_call" | custom-call | tf_op jit(solution)/shard_map/forward/pallas_call | solution.py:541
  24.8 3.8 %write.1 = (f32[19,8,64,128]{3,2,1,0:T(8,128)}, f32[19,8,64,128]{3,2,1,0:T(8,128)}) custom-call(f32[19,8,64,128]{3,2,1,0:T(8,128)S(1)} %get-tuple-element.7.state_in, f32[19,8,64,128]{3,2,1,0:T(8,128)S(1)} %get-tuple-element.8.adjoint_in, f32[19,10,80,128]{3,2,1,0:T(8,128)S(1)} %get-tuple-element.9.post, f32[19,10,80,128]{3,2,1,0:T(8,128)S(1)} %get-tuple-element.10.held, ...), custom_call_target="tpu_custom_call" | custom-call | tf_op jit(solution)/shard_map/write/pallas_call | solution.py:569
